TPU v7x, 128 devices: a whole 4x4x4 slice. The times are simulated.
128 devices in a mesh: col: 128 (over z, x, y, core).
Axes of the slice: x: 4, y: 4, z: 4, core: 2. Of those that a mesh axis runs over, the one named last changes fastest.
Arguments:
- covariance: float32 [2, 8192, 8192], P(None, 'col'), may hold values from -6 to 6, as said below
- forcing: float32 [2, 8192, 8192], P(None, 'col'), may hold values from -24 to 24, as said below
- coefficient: float32 [2, 64, 128], replicated, may hold values from 0.5 to 1.5
- y_operator: float32 [2, 64, 64], replicated, may hold values from -0.75 to 0.75
- z_operator: float32 [2, 128, 128], replicated, may hold values from -0.5 to 0.5
Outputs:
- advanced: float32 [2, 8192, 8192], P(None, 'col')
Inputs may be any that keep to these rules, and one draw needn't show every extreme that they name: Each harmonic's covariance is symmetric. Each harmonic's forcing is symmetric.
All inputs are finite; a program needn't handle non-finite values.
Results may differ from a plain program's by a relative error of at most 0.0001.
Values sent between devices are 32-bit elements; how exact they have to be, the bound alone decides.
A program may use at most 192 MiB of HBM per device.

v0:
```python
import jax
import jax.numpy as jnp
from jax import lax
from jax.sharding import PartitionSpec as P

step_size = 0.2


def combined(values, y_operator, z_operator):
    along_y = jnp.einsum("hya,hacz->hycz", y_operator, values, precision=lax.Precision.HIGHEST)
    along_z = jnp.einsum("hycb,hzb->hycz", values, z_operator, precision=lax.Precision.HIGHEST)
    return along_y + along_z


def apply_operator(row_slab, y_operator, z_operator, coefficient):
    grid_y = y_operator.shape[1]
    grid_z = z_operator.shape[1]
    width = row_slab.shape[1]
    grid = jnp.swapaxes(row_slab.reshape(2, width, grid_y, grid_z), 1, 2)
    inner = coefficient[:, :, None, :] * combined(grid, y_operator, z_operator)
    outer = combined(inner, y_operator, z_operator)
    return jnp.swapaxes(outer, 1, 2).reshape(row_slab.shape)


def transpose_slab(product):
    width = product.shape[1]
    groups = lax.axis_size("col")
    received = lax.all_to_all(product, "col", split_axis=2, concat_axis=2, tiled=True)
    blocks = received.reshape(2, width, groups, width)
    return jnp.swapaxes(blocks, 1, 3).reshape(2, width, groups * width)


def on_device(covariance, forcing, coefficient, y_operator, z_operator):

    def slope_of(state):
        product = apply_operator(state, y_operator, z_operator, coefficient)
        return product + transpose_slab(product) + forcing

    slope_one = slope_of(covariance)
    slope_two = slope_of(covariance + 0.5 * step_size * slope_one)
    slope_three = slope_of(covariance + 0.5 * step_size * slope_two)
    slope_four = slope_of(covariance + step_size * slope_three)
    return covariance + step_size / 6.0 * (
        slope_one + 2.0 * slope_two + 2.0 * slope_three + slope_four
    )


def solution(mesh):
    placed = (P(None, "col", None), P(None, "col", None), P(), P(), P())
    return jax.shard_map(
        on_device, mesh=mesh, in_specs=placed, out_specs=P(None, "col", None), check_vma=False
    )
```

profile of v0, /device:TPU:1, one launch (start us, length us, event | category | flops | bytes accessed | tf_op | source)
XLA Modules:
  0.0 633.6 jit_solution(9977666709495905818)
XLA Ops:
  24.9 10.8 %copy.57 = f32[2,64,8192]{1,0,2:T(2,128)} copy(f32[2,64,8192]{2,1,0:T(8,128)} %reshape.50) | data formatting | bytes 8388608 | tf_op jit(solution)/shard_map/reshape | solution.py:22
  35.7 11.1 %reshape.67 = f32[128,1,8192]{2,1,0:T(1,128)} reshape(f32[8192,2,64]{2,1,0:T(2,128)} %bitcast.207) | data formatting | bytes 8388608
  46.8 64.8 %all_to_all.20 = f32[128,1,8192]{2,1,0:T(1,128)} all-to-all(f32[128,1,8192]{2,1,0:T(1,128)} %reshape.67), channel_id=1, replica_groups=mesh['col'=128] {'col'}, dimensions={0} | all-to-all | bytes 8388608 | tf_op jit(solution)/shard_map/all_to_all | solution.py:28
  112.1 13.8 %reduce = f32[128,8192]{1,0:T(8,128)} reduce(f32[128,1,8192]{2,1,0:T(1,128)} %all_to_all.20, f32[]{:T(128)} %broadcast.12), dimensions={1}, to_apply=%all_to_all.12.reduce_sub_computation | reduce | bytes 8388612 | tf_op jit(solution)/shard_map/all_to_all | solution.py:28
  125.8 9.6 %reshape.68 = f32[8192,2,64]{2,1,0:T(2,128)} reshape(f32[128,8192]{1,0:T(8,128)} %reduce) | data formatting | bytes 8388608
  135.4 11.4 %copy.107 = f32[2,64,128,64]{1,2,3,0:T(8,128)} copy(f32[2,64,128,64]{1,0,3,2:T(2,128)} %bitcast.211) | data formatting | bytes 8388608 | tf_op jit(solution)/shard_map/transpose | solution.py:30
  185.3 10.8 %copy.63 = f32[2,64,8192]{1,0,2:T(2,128)} copy(f32[2,64,8192]{2,1,0:T(8,128)} %reshape.54) | data formatting | bytes 8388608 | tf_op jit(solution)/shard_map/reshape | solution.py:22
  196.0 11.1 %reshape.69 = f32[128,1,8192]{2,1,0:T(1,128)} reshape(f32[8192,2,64]{2,1,0:T(2,128)} %bitcast.208) | data formatting | bytes 8388608
  207.2 59.0 %all_to_all.21 = f32[128,1,8192]{2,1,0:T(1,128)} all-to-all(f32[128,1,8192]{2,1,0:T(1,128)} %reshape.69), channel_id=1, replica_groups=mesh['col'=128] {'col'}, dimensions={0} | all-to-all | bytes 8388608 | tf_op jit(solution)/shard_map/all_to_all | solution.py:28
  266.2 13.7 %reduce.1 = f32[128,8192]{1,0:T(8,128)} reduce(f32[128,1,8192]{2,1,0:T(1,128)} %all_to_all.21, f32[]{:T(128)} %broadcast.12), dimensions={1}, to_apply=%all_to_all.13.reduce_sub_computation | reduce | bytes 8388612 | tf_op jit(solution)/shard_map/all_to_all | solution.py:28
  279.9 9.6 %reshape.70 = f32[8192,2,64]{2,1,0:T(2,128)} reshape(f32[128,8192]{1,0:T(8,128)} %reduce.1) | data formatting | bytes 8388608
  289.4 11.4 %copy.106 = f32[2,64,128,64]{1,2,3,0:T(8,128)} copy(f32[2,64,128,64]{1,0,3,2:T(2,128)} %bitcast.213) | data formatting | bytes 8388608 | tf_op jit(solution)/shard_map/transpose | solution.py:30
  339.3 10.8 %copy.69 = f32[2,64,8192]{1,0,2:T(2,128)} copy(f32[2,64,8192]{2,1,0:T(8,128)} %reshape.58) | data formatting | bytes 8388608 | tf_op jit(solution)/shard_map/reshape | solution.py:22
  350.1 11.1 %reshape.71 = f32[128,1,8192]{2,1,0:T(1,128)} reshape(f32[8192,2,64]{2,1,0:T(2,128)} %bitcast.209) | data formatting | bytes 8388608
  361.2 59.0 %all_to_all.22 = f32[128,1,8192]{2,1,0:T(1,128)} all-to-all(f32[128,1,8192]{2,1,0:T(1,128)} %reshape.71), channel_id=1, replica_groups=mesh['col'=128] {'col'}, dimensions={0} | all-to-all | bytes 8388608 | tf_op jit(solution)/shard_map/all_to_all | solution.py:28
  420.2 13.7 %reduce.2 = f32[128,8192]{1,0:T(8,128)} reduce(f32[128,1,8192]{2,1,0:T(1,128)} %all_to_all.22, f32[]{:T(128)} %broadcast.12), dimensions={1}, to_apply=%all_to_all.14.reduce_sub_computation | reduce | bytes 8388612 | tf_op jit(solution)/shard_map/all_to_all | solution.py:28
  434.0 9.6 %reshape.72 = f32[8192,2,64]{2,1,0:T(2,128)} reshape(f32[128,8192]{1,0:T(8,128)} %reduce.2) | data formatting | bytes 8388608
  443.5 11.4 %copy.105 = f32[2,64,128,64]{1,2,3,0:T(8,128)} copy(f32[2,64,128,64]{1,0,3,2:T(2,128)} %bitcast.215) | data formatting | bytes 8388608 | tf_op jit(solution)/shard_map/transpose | solution.py:30
  493.4 10.8 %copy.75 = f32[2,64,8192]{1,0,2:T(2,128)} copy(f32[2,64,8192]{2,1,0:T(8,128)} %reshape.62) | data formatting | bytes 8388608 | tf_op jit(solution)/shard_map/reshape | solution.py:22
  504.2 11.1 %reshape.73 = f32[128,1,8192]{2,1,0:T(1,128)} reshape(f32[8192,2,64]{2,1,0:T(2,128)} %bitcast.210) | data formatting | bytes 8388608
  515.3 58.5 %all_to_all.23 = f32[128,1,8192]{2,1,0:T(1,128)} all-to-all(f32[128,1,8192]{2,1,0:T(1,128)} %reshape.73), channel_id=1, replica_groups=mesh['col'=128] {'col'}, dimensions={0} | all-to-all | bytes 8388608 | tf_op jit(solution)/shard_map/all_to_all | solution.py:28
  573.9 13.7 %reduce.3 = f32[128,8192]{1,0:T(8,128)} reduce(f32[128,1,8192]{2,1,0:T(1,128)} %all_to_all.23, f32[]{:T(128)} %broadcast.12), dimensions={1}, to_apply=%all_to_all.15.reduce_sub_computation | reduce | bytes 8388612 | tf_op jit(solution)/shard_map/all_to_all | solution.py:28
  597.2 11.4 %copy.104 = f32[2,64,128,64]{1,2,3,0:T(8,128)} copy(f32[2,64,128,64]{1,0,3,2:T(2,128)} %bitcast.217) | data formatting | bytes 8388608 | tf_op jit(solution)/shard_map/transpose | solution.py:30
  616.5 16.8 %multiply_add_fusion = f32[2,64,8192]{2,1,0:T(8,128)} fusion(f32[2,64,8192]{2,1,0:T(8,128)} %param.5, f32[2,64,8192]{2,1,0:T(8,128)} %param.6, f32[2,64,8192]{2,1,0:T(8,128)} %reshape.62, f32[2,64,8192]{2,1,0:T(8,128)} %reshape.64, f32[2,64,8192]{2,1,0:T(8,128)} %reshape.50, f32[2,64,8192]{2,1,0:T(8,128)} %reshape.52, f32[2,64,8192]{2,1,0:T(8,128)} %reshape.54, ...), kind=kLoop, calls=%fused_computation.26 | loop fusion | flops 15728640 | bytes 46137344 | tf_op jit(solution)/shard_map/add | solution.py:43
  (39 shorter events, 157.9 us)
Async XLA Ops:
  0.0 3.0 copy-start
  3.0 3.7 copy-start.1
  3.0 3.7 copy-start.2
where the time goes:
time: 646 us; the launch traced here: 634 us
  blocking collectives  241 us (37%)
  local copies, waits for them, and re-layouts  229 us (35%)
  other arithmetic  92.6 us (14%)
  matrix products  70 us (11%)
    all_to_all x4, blocking collectives, transpose_slab(): lax.all_to_all(product, 'col', split_axis=2, concat_axis=2, tiled=True)  241 us
    unnamed x18, local copies, waits for them, and re-layouts  88 us
    reshape x8, local copies, waits for them, and re-layouts, apply_operator(): return jnp.swapaxes(outer, 1, 2).reshape(row_slab.shape)  62.9 us
    all_to_all x4, other arithmetic, transpose_slab(): lax.all_to_all(product, 'col', split_axis=2, concat_axis=2, tiled=True)  55 us
    transpose x4, local copies, waits for them, and re-layouts, transpose_slab(): return jnp.swapaxes(blocks, 1, 3).reshape(2, width, groups * width)  45.8 us
    dot_general x8, matrix products, combined(): jnp.einsum('hycb,hzb->hycz', values, z_operator, precision=lax.Precision....  35.4 us
    dot_general x8, matrix products, combined(): jnp.einsum('hya,hacz->hycz', y_operator, values, precision=lax.Precision....  34.6 us
    reshape x4, local copies, waits for them, and re-layouts, transpose_slab(): return jnp.swapaxes(blocks, 1, 3).reshape(2, width, groups * width)  32 us

commit v1 on v0

v1 whole, which is shorter than its diff:
```python
import functools

import jax
import jax.numpy as jnp
from jax import lax
from jax.experimental import pallas as pl
from jax.experimental.pallas import tpu as pltpu
from jax.sharding import PartitionSpec as P

MESH = pl.DeviceIdType.MESH

step_size = 0.2

LINES = 64
WIDTH = 128
ROWS = 64
SLAB = LINES * ROWS
DEVICES = 128


def split(values):
    high = values.astype(jnp.bfloat16)
    low = (values - high.astype(jnp.float32)).astype(jnp.bfloat16)
    return high, low


def kernel(
    covariance, forcing, coefficient, y_tiled, z_operator, advanced,
    held_c, held_g, held_w, held_p, inner, along_y, outbox, inbox, y_factor, z_factor,
    load_sem, store_sem, send_sem, recv_sem,
):
    me = lax.axis_index("col")
    chip = me // 2
    place_z, place_x, place_y = chip // 16, (chip // 4) % 4, chip % 4

    barrier = pltpu.get_barrier_semaphore()

    def greet(step, carry):
        pl.semaphore_signal(
            barrier, inc=1, device_id=(lax.rem(me + step, DEVICES),), device_id_type=MESH
        )
        return carry

    lax.fori_loop(1, DEVICES, greet, 0)

    def load(source, target, sem, h):
        def line(y, carry):
            pltpu.make_async_copy(
                source.at[h, :, pl.ds(pl.multiple_of(y * WIDTH, WIDTH), WIDTH)],
                target.at[h, pl.ds(pl.multiple_of(y * ROWS, ROWS), ROWS), :],
                sem,
            ).start()
            return carry

        lax.fori_loop(0, LINES, line, 0)

    def wait_load(target, sem, h):
        pltpu.make_async_copy(target.at[h], target.at[h], sem).wait()

    for h in range(2):
        load(covariance, held_c, load_sem.at[0, h], h)
    for h in range(2):
        load(forcing, held_g, load_sem.at[1, h], h)

    lane = lax.broadcasted_iota(jnp.int32, (32, WIDTH), 1)
    left_half = lane < 64

    for h in range(2):
        tiled = y_tiled[h]
        high, low = split(tiled)
        first = lax.broadcasted_iota(jnp.int32, tiled.shape, 1) < 128
        y_factor[h] = jnp.where(first, high.astype(jnp.float32), low.astype(jnp.float32)).astype(
            jnp.bfloat16
        )
        high, low = split(z_operator[h].T)
        z_factor[h, 0:128, 0:128] = high
        z_factor[h, 0:128, 128:256] = low
        z_factor[h, 128:256, 0:128] = high
        z_factor[h, 128:256, 128:256] = jnp.zeros_like(low)

    def contract_y(source, h):
        factor = y_factor[h]

        def pair(j, carry):
            row = j * 2
            both = jnp.concatenate(
                [source[pl.ds(row + k, LINES, stride=ROWS), :] for k in range(2)], axis=1
            )
            high, low = split(both)
            stacked = jnp.concatenate([high, low, high, low], axis=0)
            out = jnp.dot(factor, stacked, preferred_element_type=jnp.float32)
            for k in range(2):
                along_y[pl.ds(row + k, LINES, stride=ROWS), :] = out[:, k * 128 : (k + 1) * 128]
            return carry

        lax.fori_loop(0, ROWS // 2, pair, 0, unroll=4)

    def combined(source, h, y):
        rows = pl.ds(pl.multiple_of(y * ROWS, ROWS), ROWS)
        high, low = split(source[rows, :])
        out = jnp.dot(
            jnp.concatenate([high, low], axis=1), z_factor[h], preferred_element_type=jnp.float32
        )
        return out[:, 0:128] + out[:, 128:256] + along_y[rows, :]

    def first_half(source, h):
        contract_y(source, h)

        def line(y, carry):
            gain = step_size * coefficient[h, pl.ds(y, 1), :]
            inner[pl.ds(pl.multiple_of(y * ROWS, ROWS), ROWS), :] = gain * combined(source, h, y)
            return carry

        lax.fori_loop(0, LINES, line, 0, unroll=4)
        contract_y(inner, h)

    def target_line(q):
        u, v, w = q % 4, (q // 4) % 4, q // 16
        return (
            ((place_z + u) % 4) * 16 + ((place_x + u + v) % 4) * 4 + (place_y + u + v + w) % 4
        )

    def post(exchange, h, lines, values):
        turned = jnp.concatenate(values, axis=0).T
        for core in range(2):
            upper = turned[core * 64 : core * 64 + 32]
            lower = turned[core * 64 + 32 : core * 64 + 64]
            blocks = (
                jnp.where(left_half, upper, pltpu.roll(lower, 64, 1)),
                jnp.where(left_half, pltpu.roll(upper, 64, 1), lower),
            )
            for k in range(2):
                device = lines[k] * 2 + core
                outbox[h, device] = blocks[k]

                @pl.when(device == me)
                def _():
                    inbox[exchange, h, device] = blocks[k]

                @pl.when(device != me)
                def _():
                    pltpu.make_async_remote_copy(
                        src_ref=outbox.at[h, device],
                        dst_ref=inbox.at[exchange, h, me],
                        send_sem=send_sem.at[exchange, h],
                        recv_sem=recv_sem.at[exchange, h],
                        device_id=(device,),
                        device_id_type=MESH,
                    ).start()

    def post_all(exchange, h, value_of):
        def pair(s, carry):
            lines = [target_line(2 * s), target_line(2 * s + 1)]
            post(exchange, h, lines, [value_of(y) for y in lines])
            return carry

        lax.fori_loop(0, LINES // 2, pair, 0)

    def everything(exchange, h):
        whole = inbox.at[exchange, h, pl.ds(0, DEVICES - 1)]
        return pltpu.make_async_remote_copy(
            src_ref=whole,
            dst_ref=whole,
            send_sem=send_sem.at[exchange, h],
            recv_sem=recv_sem.at[exchange, h],
            device_id=(lax.rem(me + 1, DEVICES),),
            device_id_type=MESH,
        )

    def arrived(exchange, h, y):
        zero, one = inbox[exchange, h, 2 * y], inbox[exchange, h, 2 * y + 1]
        return jnp.concatenate(
            [
                jnp.where(left_half, zero, pltpu.roll(one, 64, 1)),
                jnp.where(left_half, pltpu.roll(zero, 64, 1), one),
            ],
            axis=0,
        )

    def rows_of(y):
        return pl.ds(pl.multiple_of(y * ROWS, ROWS), ROWS)

    def stage_zero(h, carry):
        wait_load(held_c, load_sem.at[0, h], h)
        first_half(held_c.at[h], h)

        @pl.when(h == 0)
        def _():
            pl.semaphore_wait(barrier, DEVICES - 1)

        def value_of(y):
            value = combined(inner, h, y)
            held_w[h, rows_of(y), :] = value
            return value

        post_all(0, h, value_of)
        return carry

    lax.fori_loop(0, 2, stage_zero, 0)

    def stage_one(h, carry):
        wait_load(held_g, load_sem.at[1, h], h)
        everything(0, h).wait()

        def gather(y, carry):
            rows = rows_of(y)
            held_g[h, rows, :] = (
                step_size * held_g[h, rows, :] + held_w[h, rows, :] + arrived(0, h, y)
            )
            return carry

        lax.fori_loop(0, LINES, gather, 0, unroll=2)
        first_half(held_g.at[h], h)

        def line(y, carry):
            held_w[h, rows_of(y), :] = combined(inner, h, y)
            return carry

        lax.fori_loop(0, LINES, line, 0, unroll=4)
        first_half(held_w.at[h], h)

        def value_of(y):
            rows = rows_of(y)
            second = combined(inner, h, y)
            held_p[h, rows, :] = second
            return second + (4.0 / 3.0) * held_w[h, rows, :]

        post_all(1, h, value_of)
        return carry

    lax.fori_loop(0, 2, stage_one, 0)

    def stage_between(h, carry):
        first_half(held_p.at[h], h)

        def line(y, carry):
            rows = rows_of(y)
            third = combined(inner, h, y) * (1.0 / 24.0)
            one = held_w[h, rows, :]
            held_c[h, rows, :] = (
                held_c[h, rows, :]
                + held_g[h, rows, :]
                + 0.5 * one
                + (1.0 / 6.0) * held_p[h, rows, :]
                + third
            )
            held_w[h, rows, :] = (5.0 / 18.0) * one + third
            return carry

        lax.fori_loop(0, LINES, line, 0, unroll=2)
        return carry

    lax.fori_loop(0, 2, stage_between, 0)

    def stage_two(h, carry):
        everything(1, h).wait()

        def gather(y, carry):
            held_p[h, rows_of(y), :] = arrived(1, h, y)
            return carry

        lax.fori_loop(0, LINES, gather, 0, unroll=2)
        first_half(held_p.at[h], h)

        def value_of(y):
            rows = rows_of(y)
            eighth = 0.125 * combined(inner, h, y)
            held_c[h, rows, :] = held_c[h, rows, :] + (1.0 / 6.0) * held_p[h, rows, :] + eighth
            return held_w[h, rows, :] + eighth

        post_all(2, h, value_of)
        return carry

    lax.fori_loop(0, 2, stage_two, 0)

    def stage_last(h, carry):
        everything(2, h).wait()

        def line(y, carry):
            rows = rows_of(y)
            held_g[h, rows, :] = held_c[h, rows, :] + arrived(2, h, y)
            pltpu.make_async_copy(
                held_g.at[h, rows, :],
                advanced.at[h, :, pl.ds(pl.multiple_of(y * WIDTH, WIDTH), WIDTH)],
                store_sem.at[h],
            ).start()
            return carry

        lax.fori_loop(0, LINES, line, 0, unroll=2)
        return carry

    lax.fori_loop(0, 2, stage_last, 0)
    for h in range(2):
        wait_load(held_g, store_sem.at[h], h)


def on_device(covariance, forcing, coefficient, y_operator, z_operator):
    slab = pltpu.VMEM((2, SLAB, WIDTH), jnp.float32)
    part = pltpu.VMEM((SLAB, WIDTH), jnp.float32)
    hbm = pl.BlockSpec(memory_space=pl.ANY)
    vmem = pl.BlockSpec(memory_space=pltpu.VMEM)
    return pl.pallas_call(
        kernel,
        out_shape=jax.ShapeDtypeStruct(covariance.shape, jnp.float32),
        in_specs=[hbm, hbm, vmem, vmem, vmem],
        out_specs=hbm,
        scratch_shapes=[
            slab, slab, slab, slab, part, part,
            pltpu.VMEM((2, DEVICES, 32, WIDTH), jnp.float32),
            pltpu.VMEM((3, 2, DEVICES, 32, WIDTH), jnp.float32),
            pltpu.VMEM((2, LINES, 256), jnp.bfloat16),
            pltpu.VMEM((2, 256, 256), jnp.bfloat16),
            pltpu.SemaphoreType.DMA((2, 2)),
            pltpu.SemaphoreType.DMA((2,)),
            pltpu.SemaphoreType.DMA((3, 2)),
            pltpu.SemaphoreType.DMA((3, 2)),
        ],
        compiler_params=pltpu.CompilerParams(
            collective_id=0, has_side_effects=True, vmem_limit_bytes=56 * 2**20
        ),
        cost_estimate=pl.CostEstimate(
            flops=25 * 10**9, bytes_accessed=12 * 2**20, transcendentals=0
        ),
    )(covariance, forcing, coefficient, jnp.tile(y_operator, (1, 1, 4)), z_operator)


def solution(mesh):
    placed = (P(None, "col", None), P(None, "col", None), P(), P(), P())
    return jax.shard_map(
        on_device, mesh=mesh, in_specs=placed, out_specs=P(None, "col", None), check_vma=False
    )
```

time: 646 us -> 242 us (0.37)
  the two profiles are of different devices: /device:TPU:1 before, /device:TPU:3 now
where the time goes in v1:
time: 242 us; the launch traced here: 237 us
  Pallas kernels  231 us (95%)
  local copies, waits for them, and re-layouts  6.35 us (3%)
    pallas_call x1, Pallas kernels, on_device(): pl.pallas_call(kernel, out_shape=jax.ShapeDtypeStruct(covariance.shape, j...  231 us

profile of v1, /device:TPU:3, one launch (start us, length us, event | category | flops | bytes accessed | tf_op | source)
XLA Modules:
  0.0 237.0 jit_solution(2428940188242206842)
XLA Ops:
  0.0 0.9 tile.4
  0.9 0.9 tile.10.y_tiled
  1.7 230.6 %shard_map.55 = f32[2,64,8192]{2,1,0:T(8,128)} custom-call(f32[2,64,8192]{2,1,0:T(8,128)} %covariance.1, f32[2,64,8192]{2,1,0:T(8,128)} %forcing.1, f32[2,64,128]{2,1,0:T(8,128)} %coefficient.1, f32[2,64,256]{2,1,0:T(8,128)} %tile.10.y_tiled, f32[2,128,128]{2,1,0:T(8,128)} %z_operator.1), custom_call_target="tpu_custom_call" | custom-call | flops 24999999488 | bytes 12582912 | tf_op jit(solution)/shard_map/pallas_call | solution.py:302
  232.4 4.6 %copy.7 = f32[2,64,8192]{2,1,0:T(8,128)} copy(f32[2,64,8192]{2,1,0:T(8,128)} %shard_map.55) | data formatting | bytes 8388608

commit v2 on v1

v2 whole, which is shorter than its diff:
```python
import functools

import jax
import jax.numpy as jnp
from jax import lax
from jax.experimental import pallas as pl
from jax.experimental.pallas import tpu as pltpu
from jax.sharding import PartitionSpec as P

MESH = pl.DeviceIdType.MESH

step_size = 0.2

LINES = 64
WIDTH = 128
ROWS = 64
SLAB = LINES * ROWS
DEVICES = 128


def split(values):
    high = values.astype(jnp.bfloat16)
    low = (values - high.astype(jnp.float32)).astype(jnp.bfloat16)
    return high, low


def kernel(
    covariance, forcing, coefficient, y_operator, z_operator, advanced,
    held_c, held_g, held_w, held_p, inner, outer, along_y, outbox, inbox, y_factor, z_factor,
    load_sem, store_sem, send_sem, recv_sem,
):
    me = lax.axis_index("col")
    chip = me // 2
    place_z, place_x, place_y = chip // 16, (chip // 4) % 4, chip % 4

    barrier = pltpu.get_barrier_semaphore()

    def greet(step, carry):
        pl.semaphore_signal(
            barrier, inc=1, device_id=(lax.rem(me + step, DEVICES),), device_id_type=MESH
        )
        return carry

    lax.fori_loop(1, DEVICES, greet, 0)

    def load(source, target, sem, h):
        def line(y, carry):
            pltpu.make_async_copy(
                source.at[h, :, pl.ds(pl.multiple_of(y * WIDTH, WIDTH), WIDTH)],
                target.at[h, pl.ds(pl.multiple_of(y * ROWS, ROWS), ROWS), :],
                sem,
            ).start()
            return carry

        lax.fori_loop(0, LINES, line, 0)

    def wait_load(target, sem, h):
        pltpu.make_async_copy(target.at[h], target.at[h], sem).wait()

    for h in range(2):
        load(covariance, held_c, load_sem.at[0, h], h)
    for h in range(2):
        load(forcing, held_g, load_sem.at[1, h], h)

    def rows_of(y):
        return pl.ds(pl.multiple_of(y * ROWS, ROWS), ROWS)

    lane = lax.broadcasted_iota(jnp.int32, (32, WIDTH), 1)
    left_half = lane < 64

    for h in range(2):
        high, low = split(y_operator[h])
        pieces = [half.astype(jnp.float32) for half in (high, high, low, low)]
        y_factor[h] = jnp.concatenate(pieces, axis=1).astype(jnp.bfloat16)
        high, low = split(z_operator[h].T)
        z_factor[h, 0:128, 0:128] = high
        z_factor[h, 0:128, 128:256] = low
        z_factor[h, 128:256, 0:128] = high
        z_factor[h, 128:256, 128:256] = jnp.zeros_like(low)

    def contract_y(source, h):
        group = 16
        factor = y_factor[h]

        def step(j, carry):
            row = j * group
            both = jnp.concatenate(
                [source[pl.ds(row + k, LINES, stride=ROWS), :] for k in range(group)], axis=1
            )
            high, low = split(both)
            stacked = jnp.concatenate([high, low, high, low], axis=0)
            out = jnp.dot(factor, stacked, preferred_element_type=jnp.float32)
            for k in range(group):
                along_y[pl.ds(row + k, LINES, stride=ROWS), :] = out[:, k * 128 : (k + 1) * 128]
            return carry

        lax.fori_loop(0, ROWS // group, step, 0, unroll=2)

    def combined(source, h, write):
        group = 32

        def step(j, carry):
            rows = pl.ds(pl.multiple_of(j * (group * ROWS), group * ROWS), group * ROWS)
            high, low = split(source[rows, :])
            out = jnp.dot(
                jnp.concatenate([high, low], axis=1),
                z_factor[h],
                preferred_element_type=jnp.float32,
            )
            value = out[:, 0:128] + out[:, 128:256] + along_y[rows, :]
            for k in range(group):
                write(j * group + k, value[k * ROWS : (k + 1) * ROWS])
            return carry

        lax.fori_loop(0, LINES // group, step, 0)

    def first_half(source, h):
        contract_y(source, h)

        def write(y, value):
            inner[rows_of(y), :] = (step_size * coefficient[h, pl.ds(y, 1), :]) * value

        combined(source, h, write)
        contract_y(inner, h)

    def target_line(q):
        u, v, w = q % 4, (q // 4) % 4, q // 16
        return (
            ((place_z + u) % 4) * 16 + ((place_x + u + v) % 4) * 4 + (place_y + u + v + w) % 4
        )

    def post(exchange, h, source):
        group = 8

        def step(s, carry):
            lines = [target_line(s * group + k) for k in range(group)]
            for k in range(0, group, 2):
                pair = [source[rows_of(y), :] for y in lines[k : k + 2]]
                turned = jnp.concatenate(pair, axis=0).T
                for core in range(2):
                    upper = turned[core * 64 : core * 64 + 32]
                    lower = turned[core * 64 + 32 : core * 64 + 64]
                    outbox[h, lines[k] * 2 + core] = jnp.where(
                        left_half, upper, pltpu.roll(lower, 64, 1)
                    )
                    outbox[h, lines[k + 1] * 2 + core] = jnp.where(
                        left_half, pltpu.roll(upper, 64, 1), lower
                    )

            def send(device):
                pltpu.make_async_remote_copy(
                    src_ref=outbox.at[h, device],
                    dst_ref=inbox.at[exchange, h, me],
                    send_sem=send_sem.at[exchange, h],
                    recv_sem=recv_sem.at[exchange, h],
                    device_id=(device,),
                    device_id_type=MESH,
                ).start()

            for k in range(group):
                if k > 0:
                    for core in range(2):
                        send(lines[k] * 2 + core)
                else:

                    @pl.when(s > 0)
                    def _():
                        for core in range(2):
                            send(lines[0] * 2 + core)

                    @pl.when(s == 0)
                    def _():
                        send(me + 1 - 2 * lax.rem(me, 2))

            return carry

        lax.fori_loop(0, LINES // group, step, 0)
        inbox[exchange, h, me] = outbox[h, me]

    def everything(exchange, h):
        whole = inbox.at[exchange, h, pl.ds(0, DEVICES - 1)]
        return pltpu.make_async_remote_copy(
            src_ref=whole,
            dst_ref=whole,
            send_sem=send_sem.at[exchange, h],
            recv_sem=recv_sem.at[exchange, h],
            device_id=(lax.rem(me + 1, DEVICES),),
            device_id_type=MESH,
        )

    def arrived(exchange, h, y):
        zero, one = inbox[exchange, h, 2 * y], inbox[exchange, h, 2 * y + 1]
        return jnp.concatenate(
            [
                jnp.where(left_half, zero, pltpu.roll(one, 64, 1)),
                jnp.where(left_half, pltpu.roll(zero, 64, 1), one),
            ],
            axis=0,
        )

    def stage_zero(h):
        wait_load(held_c, load_sem.at[0, h], h)
        first_half(held_c.at[h], h)

        def write(y, value):
            held_w[h, rows_of(y), :] = value

        combined(inner, h, write)
        if h == 0:
            pl.semaphore_wait(barrier, DEVICES - 1)
        post(0, h, held_w.at[h])

    def stage_one(h):
        wait_load(held_g, load_sem.at[1, h], h)
        everything(0, h).wait()

        def gather(y, carry):
            rows = rows_of(y)
            held_g[h, rows, :] = (
                step_size * held_g[h, rows, :] + held_w[h, rows, :] + arrived(0, h, y)
            )
            return carry

        lax.fori_loop(0, LINES, gather, 0, unroll=8)
        first_half(held_g.at[h], h)

        def write_one(y, value):
            held_w[h, rows_of(y), :] = value

        combined(inner, h, write_one)
        first_half(held_w.at[h], h)

        def write_two(y, value):
            held_p[h, rows_of(y), :] = value
            outer[rows_of(y), :] = value + (4.0 / 3.0) * held_w[h, rows_of(y), :]

        combined(inner, h, write_two)
        post(1, h, outer)

    def stage_between(h):
        first_half(held_p.at[h], h)

        def write(y, value):
            rows = rows_of(y)
            third = value * (1.0 / 24.0)
            one = held_w[h, rows, :]
            held_c[h, rows, :] = (
                held_c[h, rows, :]
                + held_g[h, rows, :]
                + 0.5 * one
                + (1.0 / 6.0) * held_p[h, rows, :]
                + third
            )
            held_w[h, rows, :] = (5.0 / 18.0) * one + third

        combined(inner, h, write)

    def stage_two(h):
        everything(1, h).wait()

        def gather(y, carry):
            held_p[h, rows_of(y), :] = arrived(1, h, y)
            return carry

        lax.fori_loop(0, LINES, gather, 0, unroll=8)
        first_half(held_p.at[h], h)

        def write(y, value):
            rows = rows_of(y)
            eighth = 0.125 * value
            held_c[h, rows, :] = held_c[h, rows, :] + (1.0 / 6.0) * held_p[h, rows, :] + eighth
            outer[rows, :] = held_w[h, rows, :] + eighth

        combined(inner, h, write)
        post(2, h, outer)

    def stage_last(h):
        everything(2, h).wait()

        def group(g, carry):
            for k in range(8):
                rows = rows_of(g * 8 + k)
                held_g[h, rows, :] = held_c[h, rows, :] + arrived(2, h, g * 8 + k)
            for k in range(8):
                y = g * 8 + k
                pltpu.make_async_copy(
                    held_g.at[h, rows_of(y), :],
                    advanced.at[h, :, pl.ds(pl.multiple_of(y * WIDTH, WIDTH), WIDTH)],
                    store_sem.at[h],
                ).start()
            return carry

        lax.fori_loop(0, LINES // 8, group, 0)

    for stage in (stage_zero, stage_one, stage_between, stage_two, stage_last):
        for h in range(2):
            stage(h)
    for h in range(2):
        wait_load(held_g, store_sem.at[h], h)


def on_device(covariance, forcing, coefficient, y_operator, z_operator):
    slab = pltpu.VMEM((2, SLAB, WIDTH), jnp.float32)
    part = pltpu.VMEM((SLAB, WIDTH), jnp.float32)
    hbm = pl.BlockSpec(memory_space=pl.ANY)
    vmem = pl.BlockSpec(memory_space=pltpu.VMEM)
    return pl.pallas_call(
        kernel,
        out_shape=jax.ShapeDtypeStruct(covariance.shape, jnp.float32),
        in_specs=[hbm, hbm, vmem, vmem, vmem],
        out_specs=hbm,
        scratch_shapes=[
            slab, slab, slab, slab, part, part, part,
            pltpu.VMEM((2, DEVICES, 32, WIDTH), jnp.float32),
            pltpu.VMEM((3, 2, DEVICES, 32, WIDTH), jnp.float32),
            pltpu.VMEM((2, LINES, 256), jnp.bfloat16),
            pltpu.VMEM((2, 256, 256), jnp.bfloat16),
            pltpu.SemaphoreType.DMA((2, 2)),
            pltpu.SemaphoreType.DMA((2,)),
            pltpu.SemaphoreType.DMA((3, 2)),
            pltpu.SemaphoreType.DMA((3, 2)),
        ],
        compiler_params=pltpu.CompilerParams(
            collective_id=0, has_side_effects=True, vmem_limit_bytes=56 * 2**20
        ),
        cost_estimate=pl.CostEstimate(
            flops=25 * 10**9, bytes_accessed=12 * 2**20, transcendentals=0
        ),
    )(covariance, forcing, coefficient, y_operator, z_operator)


def solution(mesh):
    placed = (P(None, "col", None), P(None, "col", None), P(), P(), P())
    return jax.shard_map(
        on_device, mesh=mesh, in_specs=placed, out_specs=P(None, "col", None), check_vma=False
    )
```

time: 242 us -> 181 us (0.75)
  the two profiles are of different devices: /device:TPU:3 before, /device:TPU:25 now
where the time goes in v2:
time: 181 us
  Pallas kernels  176 us (97%)
  local copies, waits for them, and re-layouts  4.61 us (3%)
    pallas_call x1, Pallas kernels, on_device(): pl.pallas_call(kernel, out_shape=jax.ShapeDtypeStruct(covariance.shape, j...  176 us
    unnamed x1, local copies, waits for them, and re-layouts  4.61 us

profile of v2, /device:TPU:25, one launch (start us, length us, event | category | flops | bytes accessed | tf_op | source)
XLA Modules:
  0.0 180.7 jit_solution(2295854283838172510)
XLA Ops:
  0.0 176.1 %shard_map.55 = f32[2,64,8192]{2,1,0:T(8,128)} custom-call(f32[2,64,8192]{2,1,0:T(8,128)} %covariance.1, f32[2,64,8192]{2,1,0:T(8,128)} %forcing.1, f32[2,64,128]{2,1,0:T(8,128)} %coefficient.1, f32[2,64,64]{2,1,0:T(8,128)} %y_operator.1, f32[2,128,128]{2,1,0:T(8,128)} %z_operator.1), custom_call_target="tpu_custom_call" | custom-call | flops 24999999488 | bytes 12582912 | tf_op jit(solution)/shard_map/pallas_call | solution.py:307
  176.1 4.6 %copy.7 = f32[2,64,8192]{2,1,0:T(8,128)} copy(f32[2,64,8192]{2,1,0:T(8,128)} %shard_map.55) | data formatting | bytes 8388608

commit v3 on v2

--- a/solution.py
+++ b/solution.py
@@ -16,6 +16,8 @@
 ROWS = 64
 SLAB = LINES * ROWS
 DEVICES = 128
+AHEAD_ONE = 7
+AHEAD_TWO = 6
 
 
 def split(values):
@@ -32,6 +34,7 @@
     me = lax.axis_index("col")
     chip = me // 2
     place_z, place_x, place_y = chip // 16, (chip // 4) % 4, chip % 4
+    turn = 1 + 2 * lax.rem(me, 2)
 
     barrier = pltpu.get_barrier_semaphore()
 
@@ -124,13 +127,16 @@
         contract_y(inner, h)
 
     def target_line(q):
-        u, v, w = q % 4, (q // 4) % 4, q // 16
+        u, v, w = turn * (q % 4), turn * ((q // 4) % 4), turn * (q // 16)
         return (
-            ((place_z + u) % 4) * 16 + ((place_x + u + v) % 4) * 4 + (place_y + u + v + w) % 4
+            ((place_z + u) % 4) * 16
+            + ((place_x + 2 * u + v) % 4) * 4
+            + (place_y + u + v + w) % 4
         )
 
     def post(exchange, h, source):
         group = 8
+        box = exchange % 2
 
         def step(s, carry):
             lines = [target_line(s * group + k) for k in range(group)]
@@ -140,18 +146,18 @@
                 for core in range(2):
                     upper = turned[core * 64 : core * 64 + 32]
                     lower = turned[core * 64 + 32 : core * 64 + 64]
-                    outbox[h, lines[k] * 2 + core] = jnp.where(
+                    outbox[box, h, lines[k] * 2 + core] = jnp.where(
                         left_half, upper, pltpu.roll(lower, 64, 1)
                     )
-                    outbox[h, lines[k + 1] * 2 + core] = jnp.where(
+                    outbox[box, h, lines[k + 1] * 2 + core] = jnp.where(
                         left_half, pltpu.roll(upper, 64, 1), lower
                     )
 
             def send(device):
                 pltpu.make_async_remote_copy(
-                    src_ref=outbox.at[h, device],
+                    src_ref=outbox.at[box, h, device],
                     dst_ref=inbox.at[exchange, h, me],
-                    send_sem=send_sem.at[exchange, h],
+                    send_sem=send_sem.at[exchange, h, s],
                     recv_sem=recv_sem.at[exchange, h],
                     device_id=(device,),
                     device_id_type=MESH,
@@ -175,18 +181,25 @@
             return carry
 
         lax.fori_loop(0, LINES // group, step, 0)
-        inbox[exchange, h, me] = outbox[h, me]
-
-    def everything(exchange, h):
-        whole = inbox.at[exchange, h, pl.ds(0, DEVICES - 1)]
+        inbox[exchange, h, me] = outbox[box, h, me]
+
+    def moved(exchange, h, group, blocks):
+        part = inbox.at[exchange, h, pl.ds(0, blocks)]
         return pltpu.make_async_remote_copy(
-            src_ref=whole,
-            dst_ref=whole,
-            send_sem=send_sem.at[exchange, h],
+            src_ref=part,
+            dst_ref=part,
+            send_sem=send_sem.at[exchange, h, group],
             recv_sem=recv_sem.at[exchange, h],
             device_id=(lax.rem(me + 1, DEVICES),),
             device_id_type=MESH,
         )
+
+    def wait_sent(exchange, h, first, last):
+        for group in range(first, last):
+            moved(exchange, h, group, 16 if group else 15).wait_send()
+
+    def wait_arrived(exchange, h):
+        moved(exchange, h, 0, DEVICES - 1).wait_recv()
 
     def arrived(exchange, h, y):
         zero, one = inbox[exchange, h, 2 * y], inbox[exchange, h, 2 * y + 1]
@@ -212,12 +225,56 @@
 
     def stage_one(h):
         wait_load(held_g, load_sem.at[1, h], h)
-        everything(0, h).wait()
+
+        def start(g, carry):
+            rows = pl.ds(pl.multiple_of(g * 512, 512), 512)
+            held_g[h, rows, :] = step_size * held_g[h, rows, :] + held_w[h, rows, :]
+            return carry
+
+        lax.fori_loop(0, SLAB // 512, start, 0)
+        first_half(held_g.at[h], h)
+
+        def write(y, value):
+            held_p[h, rows_of(y), :] = value
+
+        combined(inner, h, write)
+        if h == 0:
+            post(1, h, held_p.at[h])
+
+    def stage_two(h):
+        wait_sent(0, h, 0, 8)
+        wait_arrived(0, h)
 
         def gather(y, carry):
             rows = rows_of(y)
+            value = arrived(0, h, y)
+            held_w[h, rows, :] = value
+            held_c[h, rows, :] = held_c[h, rows, :] + held_g[h, rows, :] + value
+            return carry
+
+        lax.fori_loop(0, LINES, gather, 0, unroll=8)
+        first_half(held_w.at[h], h)
+
+        def write(y, value):
+            rows = rows_of(y)
             held_g[h, rows, :] = (
-                step_size * held_g[h, rows, :] + held_w[h, rows, :] + arrived(0, h, y)
+                (1.0 / 6.0) * value
+                + (1.0 / 24.0) * held_p[h, rows, :]
+                + (1.0 / 3.0) * held_w[h, rows, :]
+            )
+
+        combined(inner, h, write)
+
+    def stage_three(h):
+        wait_arrived(1, h)
+        wait_sent(1, h, AHEAD_ONE if h == 0 else AHEAD_TWO, 8)
+
+        def gather(y, carry):
+            rows = rows_of(y)
+            value = arrived(1, h, y)
+            held_g[h, rows, :] = held_g[h, rows, :] + 0.125 * value
+            held_w[h, rows, :] = 0.5 * held_w[h, rows, :] + (1.0 / 6.0) * (
+                held_p[h, rows, :] + value
             )
             return carry
 
@@ -225,57 +282,26 @@
         first_half(held_g.at[h], h)
 
         def write_one(y, value):
-            held_w[h, rows_of(y), :] = value
+            rows = rows_of(y)
+            held_w[h, rows, :] = held_w[h, rows, :] + value
 
         combined(inner, h, write_one)
         first_half(held_w.at[h], h)
 
         def write_two(y, value):
-            held_p[h, rows_of(y), :] = value
-            outer[rows_of(y), :] = value + (4.0 / 3.0) * held_w[h, rows_of(y), :]
+            rows = rows_of(y)
+            total = value + 0.5 * held_p[h, rows, :]
+            outer[rows, :] = total
+            held_c[h, rows, :] = held_c[h, rows, :] + total
 
         combined(inner, h, write_two)
-        post(1, h, outer)
-
-    def stage_between(h):
-        first_half(held_p.at[h], h)
-
-        def write(y, value):
-            rows = rows_of(y)
-            third = value * (1.0 / 24.0)
-            one = held_w[h, rows, :]
-            held_c[h, rows, :] = (
-                held_c[h, rows, :]
-                + held_g[h, rows, :]
-                + 0.5 * one
-                + (1.0 / 6.0) * held_p[h, rows, :]
-                + third
-            )
-            held_w[h, rows, :] = (5.0 / 18.0) * one + third
-
-        combined(inner, h, write)
-
-    def stage_two(h):
-        everything(1, h).wait()
-
-        def gather(y, carry):
-            held_p[h, rows_of(y), :] = arrived(1, h, y)
-            return carry
-
-        lax.fori_loop(0, LINES, gather, 0, unroll=8)
-        first_half(held_p.at[h], h)
-
-        def write(y, value):
-            rows = rows_of(y)
-            eighth = 0.125 * value
-            held_c[h, rows, :] = held_c[h, rows, :] + (1.0 / 6.0) * held_p[h, rows, :] + eighth
-            outer[rows, :] = held_w[h, rows, :] + eighth
-
-        combined(inner, h, write)
+        if h == 0:
+            wait_sent(1, 1, 0, AHEAD_TWO)
         post(2, h, outer)
 
     def stage_last(h):
-        everything(2, h).wait()
+        wait_arrived(2, h)
+        wait_sent(2, h, 0, 8)
 
         def group(g, carry):
             for k in range(8):
@@ -292,7 +318,12 @@
 
         lax.fori_loop(0, LINES // 8, group, 0)
 
-    for stage in (stage_zero, stage_one, stage_between, stage_two, stage_last):
+    for stage in (stage_zero, stage_one, stage_two):
+        for h in range(2):
+            stage(h)
+    wait_sent(1, 0, 0, AHEAD_ONE)
+    post(1, 1, held_p.at[1])
+    for stage in (stage_three, stage_last):
         for h in range(2):
             stage(h)
     for h in range(2):
@@ -311,13 +342,13 @@
         out_specs=hbm,
         scratch_shapes=[
             slab, slab, slab, slab, part, part, part,
-            pltpu.VMEM((2, DEVICES, 32, WIDTH), jnp.float32),
+            pltpu.VMEM((2, 2, DEVICES, 32, WIDTH), jnp.float32),
             pltpu.VMEM((3, 2, DEVICES, 32, WIDTH), jnp.float32),
             pltpu.VMEM((2, LINES, 256), jnp.bfloat16),
             pltpu.VMEM((2, 256, 256), jnp.bfloat16),
             pltpu.SemaphoreType.DMA((2, 2)),
             pltpu.SemaphoreType.DMA((2,)),
-            pltpu.SemaphoreType.DMA((3, 2)),
+            pltpu.SemaphoreType.DMA((3, 2, 8)),
             pltpu.SemaphoreType.DMA((3, 2)),
         ],
         compiler_params=pltpu.CompilerParams(

time: 181 us -> 171 us (0.945)
  the two profiles are of different devices: /device:TPU:25 before, /device:TPU:3 now
where the time goes in v3:
time: 171 us
  Pallas kernels  166 us (97%)
  local copies, waits for them, and re-layouts  4.61 us (3%)
    pallas_call x1, Pallas kernels, on_device(): pl.pallas_call(kernel, out_shape=jax.ShapeDtypeStruct(covariance.shape, j...  166 us
    unnamed x1, local copies, waits for them, and re-layouts  4.61 us

profile of v3, /device:TPU:3, one launch (start us, length us, event | category | flops | bytes accessed | tf_op | source)
XLA Modules:
  0.0 170.7 jit_solution(16306390972705254419)
XLA Ops:
  0.0 166.1 %shard_map.55 = f32[2,64,8192]{2,1,0:T(8,128)} custom-call(f32[2,64,8192]{2,1,0:T(8,128)} %covariance.1, f32[2,64,8192]{2,1,0:T(8,128)} %forcing.1, f32[2,64,128]{2,1,0:T(8,128)} %coefficient.1, f32[2,64,64]{2,1,0:T(8,128)} %y_operator.1, f32[2,128,128]{2,1,0:T(8,128)} %z_operator.1), custom_call_target="tpu_custom_call" | custom-call | flops 24999999488 | bytes 12582912 | tf_op jit(solution)/shard_map/pallas_call | solution.py:338
  166.1 4.6 %copy.7 = f32[2,64,8192]{2,1,0:T(8,128)} copy(f32[2,64,8192]{2,1,0:T(8,128)} %shard_map.55) | data formatting | bytes 8388608

commit v4 on v3

--- a/solution.py
+++ b/solution.py
@@ -38,14 +38,6 @@
 
     barrier = pltpu.get_barrier_semaphore()
 
-    def greet(step, carry):
-        pl.semaphore_signal(
-            barrier, inc=1, device_id=(lax.rem(me + step, DEVICES),), device_id_type=MESH
-        )
-        return carry
-
-    lax.fori_loop(1, DEVICES, greet, 0)
-
     def load(source, target, sem, h):
         def line(y, carry):
             pltpu.make_async_copy(
@@ -60,10 +52,15 @@
     def wait_load(target, sem, h):
         pltpu.make_async_copy(target.at[h], target.at[h], sem).wait()
 
-    for h in range(2):
-        load(covariance, held_c, load_sem.at[0, h], h)
-    for h in range(2):
-        load(forcing, held_g, load_sem.at[1, h], h)
+    load(covariance, held_c, load_sem.at[0, 0], 0)
+
+    def greet(step, carry):
+        pl.semaphore_signal(
+            barrier, inc=1, device_id=(lax.rem(me + step, DEVICES),), device_id_type=MESH
+        )
+        return carry
+
+    lax.fori_loop(1, DEVICES, greet, 0)
 
     def rows_of(y):
         return pl.ds(pl.multiple_of(y * ROWS, ROWS), ROWS)
@@ -318,7 +315,12 @@
 
         lax.fori_loop(0, LINES // 8, group, 0)
 
-    for stage in (stage_zero, stage_one, stage_two):
+    stage_zero(0)
+    load(covariance, held_c, load_sem.at[0, 1], 1)
+    for h in range(2):
+        load(forcing, held_g, load_sem.at[1, h], h)
+    stage_zero(1)
+    for stage in (stage_one, stage_two):
         for h in range(2):
             stage(h)
     wait_sent(1, 0, 0, AHEAD_ONE)

time: 171 us -> 166 us (0.971)
  Pallas kernels: 166 us -> 161 us
    pallas_call x1, Pallas kernels: 166 us -> 161 us  [on_device(): pl.pallas_call(kernel, out_shape=jax.ShapeDtypeStruct(covariance.shape, j...]
where the time goes in v4:
time: 166 us; the launch traced here: 165 us
  Pallas kernels  161 us (97%)
  local copies, waits for them, and re-layouts  4.61 us (3%)
    pallas_call x1, Pallas kernels, on_device(): pl.pallas_call(kernel, out_shape=jax.ShapeDtypeStruct(covariance.shape, j...  161 us
    unnamed x1, local copies, waits for them, and re-layouts  4.61 us

profile of v4, /device:TPU:3, one launch (start us, length us, event | category | flops | bytes accessed | tf_op | source)
XLA Modules:
  0.0 165.4 jit_solution(8845531228444602651)
XLA Ops:
  0.0 160.7 %shard_map.55 = f32[2,64,8192]{2,1,0:T(8,128)} custom-call(f32[2,64,8192]{2,1,0:T(8,128)} %covariance.1, f32[2,64,8192]{2,1,0:T(8,128)} %forcing.1, f32[2,64,128]{2,1,0:T(8,128)} %coefficient.1, f32[2,64,64]{2,1,0:T(8,128)} %y_operator.1, f32[2,128,128]{2,1,0:T(8,128)} %z_operator.1), custom_call_target="tpu_custom_call" | custom-call | flops 24999999488 | bytes 12582912 | tf_op jit(solution)/shard_map/pallas_call | solution.py:340
  160.8 4.6 %copy.7 = f32[2,64,8192]{2,1,0:T(8,128)} copy(f32[2,64,8192]{2,1,0:T(8,128)} %shard_map.55) | data formatting | bytes 8388608
